TPU v7x, 32 devices: a whole 2x2x4 slice. The times are simulated.
32 devices in a mesh: layer: 4 (over z), prow: 2 (over y), pcol: 4 (over x, core).
Axes of the slice: x: 2, y: 2, z: 4, core: 2. Of those that a mesh axis runs over, the one named last changes fastest.
Arguments:
- front: bfloat16 [3072, 3072], P('prow', 'pcol')
- lower_desc: bfloat16 [3072, 2048], P('prow', 'layer')
- upper_desc: bfloat16 [2048, 3072], P('layer', 'pcol')
- pattern: int32 [4, 32], P('layer'), may hold values 0 or 1
- pivot: int32 [16, 192], P('prow'), may hold values from 0 to 191, as said below
Outputs:
- factored: float32 [3072, 3072], P('prow', 'pcol')
Inputs may be any that keep to these rules, and one draw needn't show every extreme that they name: Each row of pivot lists every offset 0 to 191 once.
All inputs are finite; a program needn't handle non-finite values. No bound on the sum of `pattern` on one device may be relied on, other than what follows from the above.
Results may differ from a plain program's by a relative error of at most 0.0003.
Values sent between devices are 32-bit elements; how exact they have to be, the bound alone decides.
A program may use at most 64 MiB of HBM per device.

v0:
```python
import jax
import jax.numpy as jnp
from jax import lax
from jax.sharding import PartitionSpec as P

KSTEP = 4
PRECISE = lax.Precision.HIGHEST


def broadcast(block, axis, holder):
    block = jnp.where(lax.axis_index(axis) == holder, block, jnp.zeros_like(block))
    return lax.psum(block, axis)


def invert_block(diagonal):
    gram = jnp.dot(diagonal.T, diagonal, precision=PRECISE)
    factor = jnp.linalg.cholesky(gram)
    return jax.scipy.linalg.cho_solve((factor, True), diagonal.T)


def shards(front, lower_desc, upper_desc, pattern, pivot):
    rows_dev, cols_dev = front.shape
    block_size = pivot.shape[1]
    grid_rows = lax.axis_size("prow")
    grid_cols = lax.axis_size("pcol")
    own_row = lax.axis_index("prow")
    own_col = lax.axis_index("pcol")
    row_blocks = rows_dev // block_size
    col_blocks = cols_dev // block_size
    step_count = KSTEP
    layer_flags = pattern[0]
    row_flags = lax.dynamic_slice_in_dim(layer_flags, own_row * row_blocks, row_blocks)
    col_flags = lax.dynamic_slice_in_dim(
        layer_flags, row_blocks * grid_rows + own_col * col_blocks, col_blocks
    )
    row_keep = jnp.repeat(row_flags, block_size).astype(jnp.bfloat16)
    col_keep = jnp.repeat(col_flags, block_size).astype(jnp.bfloat16)
    source = (jnp.arange(row_blocks, dtype=jnp.int32)[:, None] * block_size + pivot).reshape(-1)
    lower_sorted = (lower_desc * row_keep[:, None])[source]
    upper_masked = upper_desc * col_keep[None, :]
    front_sorted = front[source].astype(jnp.float32)
    row_order = jnp.repeat(
        jnp.arange(row_blocks, dtype=jnp.int32) * grid_rows + own_row, block_size
    )
    col_order = jnp.repeat(
        jnp.arange(col_blocks, dtype=jnp.int32) * grid_cols + own_col, block_size
    )
    identity = jnp.eye(block_size, dtype=jnp.float32)
    partial_value = jnp.dot(lower_sorted, upper_masked, preferred_element_type=jnp.float32)
    panel_work = front_sorted - lax.psum(partial_value, "layer")
    for step_index in range(step_count):
        root_row = step_index % grid_rows
        root_col = step_index % grid_cols
        row_start = step_index // grid_rows * block_size
        col_start = step_index // grid_cols * block_size
        rows_below = row_order > step_index
        cols_after = col_order > step_index
        block_row = panel_work[row_start : row_start + block_size, :]
        upper_row = broadcast(block_row, "prow", root_row)
        diagonal = jnp.where(
            own_col == root_col, upper_row[:, col_start : col_start + block_size], identity
        )
        column = jnp.where(
            rows_below[:, None], panel_work[:, col_start : col_start + block_size], 0.0
        )
        lower_part = jnp.dot(column, invert_block(diagonal), precision=PRECISE)
        lower_part = broadcast(lower_part, "pcol", root_col)
        product = jnp.dot(lower_part, upper_row, precision=PRECISE)
        panel_work = panel_work - jnp.where(cols_after[None, :], product, 0.0)
        current = panel_work[:, col_start : col_start + block_size]
        placed = jnp.where(rows_below[:, None] & (own_col == root_col), lower_part, current)
        panel_work = panel_work.at[:, col_start : col_start + block_size].set(placed)
    return panel_work


def solution(mesh):
    return jax.shard_map(
        shards,
        mesh=mesh,
        in_specs=(
            P("prow", "pcol"),
            P("prow", "layer"),
            P("layer", "pcol"),
            P("layer", None),
            P("prow", None),
        ),
        out_specs=P("prow", "pcol"),
        check_vma=False,
    )
```

profile of v0, /device:TPU:0, one launch (start us, length us, event | category | flops | bytes accessed | tf_op | source)
XLA Modules:
  0.0 815.6 jit_solution(1383796101373836084)
XLA Ops:
  6.5 0.9 fusion.90
  7.6 0.7 fusion.88
  8.5 0.8 broadcast_add_fusion
  9.4 2.8 broadcast_multiply_fusion
  12.2 7.2 gather_fusion.1
  19.4 5.0 fusion.7
  24.5 5.7 gather_fusion
  30.1 169.1 %all-reduce.13.cloned.1.call-done = f32[1536,768]{1,0:T(8,128)} async-done(((f32[1536,768]{1,0:T(8,128)}), f32[1536,768]{1,0:T(8,128)}) %all-reduce.13.cloned.1.call-update) | async-done | bytes 4718608 | tf_op jit(solution)/shard_map/psum | solution.py:50
  199.2 3.6 convert_subtract_fusion
  202.8 2.2 copy-done.5
  204.9 0.8 slice_select_fusion.5
  206.4 28.6 %all-reduce.15.cloned.1.call-done = f32[192,768]{1,0:T(8,128)} async-done(((f32[192,768]{1,0:T(8,128)}), f32[192,768]{1,0:T(8,128)}) %all-reduce.15.cloned.1.call-update) | async-done | bytes 589840 | tf_op jit(solution)/shard_map/psum | solution.py:12
  235.0 1.7 fusion.31
  236.8 11.7 %cholesky.228 = f32[128,128]{1,0:T(8,128)S(1)} custom-call(f32[128,128]{1,0:T(8,128)S(1)} %cholesky.376), custom_call_target="Cholesky" | custom-call | tf_op jit(solution)/shard_map/jit(cholesky)/cholesky | solution.py:17
  248.6 9.8 %custom-call.19 = f32[1,128,128]{1,2,0:T(8,128)S(1)} custom-call(f32[1,128,128]{2,1,0:T(8,128)S(1)} %get-tuple-element.100), custom_call_target="InvertDiagBlocksLowerTriangular" | custom-call | tf_op jit(solution)/shard_map/jit(cholesky)/cholesky | solution.py:17
  258.8 5.8 cholesky.248
  267.4 20.2 %custom-call.20 = f32[2,128,128]{1,2,0:T(8,128)S(1)} custom-call(f32[2,128,128]{2,1,0:T(8,128)S(1)} %pad_maximum_fusion), custom_call_target="InvertDiagBlocksLowerTriangular" | custom-call | tf_op jit(solution)/shard_map/jit(_cho_solve)/triangular_solve | solution.py:18
  289.4 4.0 convolution_select_fusion.3
  294.3 42.2 %all-reduce.17.cloned.1.call-done = f32[1536,192]{1,0:T(8,128)} async-done(((f32[1536,192]{1,0:T(8,128)}), f32[1536,192]{1,0:T(8,128)}) %all-reduce.17.cloned.1.call-update) | async-done | bytes 1179664 | tf_op jit(solution)/shard_map/psum | solution.py:12
  336.4 7.5 select_subtract_fusion.3
  343.9 2.2 copy-done.2
  346.1 0.8 select_select_fusion.3
  346.9 8.1 scatter.14
  355.1 1.9 slice_select_fusion.4
  357.4 29.9 %all-reduce.19.cloned.1.call-done = f32[192,768]{1,0:T(8,128)} async-done(((f32[192,768]{1,0:T(8,128)}), f32[192,768]{1,0:T(8,128)}) %all-reduce.19.cloned.1.call-update) | async-done | bytes 589840 | tf_op jit(solution)/shard_map/psum | solution.py:12
  387.3 1.7 fusion.33
  389.1 11.7 %cholesky.266 = f32[128,128]{1,0:T(8,128)S(1)} custom-call(f32[128,128]{1,0:T(8,128)S(1)} %cholesky.379), custom_call_target="Cholesky" | custom-call | tf_op jit(solution)/shard_map/jit(cholesky)/cholesky | solution.py:17
  400.9 9.8 %custom-call.21 = f32[1,128,128]{1,2,0:T(8,128)S(1)} custom-call(f32[1,128,128]{2,1,0:T(8,128)S(1)} %get-tuple-element.98), custom_call_target="InvertDiagBlocksLowerTriangular" | custom-call | tf_op jit(solution)/shard_map/jit(cholesky)/cholesky | solution.py:17
  411.1 5.8 cholesky.286
  417.0 0.7 compare_reduce_fusion.4
  419.7 19.9 %custom-call.22 = f32[2,128,128]{1,2,0:T(8,128)S(1)} custom-call(f32[2,128,128]{2,1,0:T(8,128)S(1)} %pad_maximum_fusion.1), custom_call_target="InvertDiagBlocksLowerTriangular" | custom-call | tf_op jit(solution)/shard_map/jit(_cho_solve)/triangular_solve | solution.py:18
  441.4 2.6 convolution_select_fusion.2
  444.2 42.8 %all-reduce.21.cloned.1.call-done = f32[1536,192]{1,0:T(8,128)} async-done(((f32[1536,192]{1,0:T(8,128)}), f32[1536,192]{1,0:T(8,128)}) %all-reduce.21.cloned.1.call-update) | async-done | bytes 1179664 | tf_op jit(solution)/shard_map/psum | solution.py:12
  487.0 7.5 select_subtract_fusion.2
  494.5 2.2 copy-done.3
  496.7 0.8 select_select_fusion.2
  497.5 8.1 scatter.15
  505.7 1.9 slice_select_fusion.3
  508.1 29.8 %all-reduce.23.cloned.1.call-done = f32[192,768]{1,0:T(8,128)} async-done(((f32[192,768]{1,0:T(8,128)}), f32[192,768]{1,0:T(8,128)}) %all-reduce.23.cloned.1.call-update) | async-done | bytes 589840 | tf_op jit(solution)/shard_map/psum | solution.py:12
  537.9 1.7 fusion.35
  539.7 11.7 %cholesky.304 = f32[128,128]{1,0:T(8,128)S(1)} custom-call(f32[128,128]{1,0:T(8,128)S(1)} %cholesky.382), custom_call_target="Cholesky" | custom-call | tf_op jit(solution)/shard_map/jit(cholesky)/cholesky | solution.py:17
  551.5 9.8 %custom-call.23 = f32[1,128,128]{1,2,0:T(8,128)S(1)} custom-call(f32[1,128,128]{2,1,0:T(8,128)S(1)} %get-tuple-element.96), custom_call_target="InvertDiagBlocksLowerTriangular" | custom-call | tf_op jit(solution)/shard_map/jit(cholesky)/cholesky | solution.py:17
  561.7 5.8 cholesky.324
  567.5 0.7 compare_reduce_fusion.2
  570.3 20.1 %custom-call.24 = f32[2,128,128]{1,2,0:T(8,128)S(1)} custom-call(f32[2,128,128]{2,1,0:T(8,128)S(1)} %pad_maximum_fusion.2), custom_call_target="InvertDiagBlocksLowerTriangular" | custom-call | tf_op jit(solution)/shard_map/jit(_cho_solve)/triangular_solve | solution.py:18
  592.2 2.6 convolution_select_fusion.1
  595.1 42.8 %all-reduce.25.cloned.1.call-done = f32[1536,192]{1,0:T(8,128)} async-done(((f32[1536,192]{1,0:T(8,128)}), f32[1536,192]{1,0:T(8,128)}) %all-reduce.25.cloned.1.call-update) | async-done | bytes 1179664 | tf_op jit(solution)/shard_map/psum | solution.py:12
  637.8 7.5 select_subtract_fusion.1
  645.3 2.2 copy-done.4
  647.5 0.8 select_select_fusion.1
  648.3 8.1 scatter.16
  656.5 1.9 slice_select_fusion.2
  658.8 29.9 %all-reduce.27.cloned.1.call-done = f32[192,768]{1,0:T(8,128)} async-done(((f32[192,768]{1,0:T(8,128)}), f32[192,768]{1,0:T(8,128)}) %all-reduce.27.cloned.1.call-update) | async-done | bytes 589840 | tf_op jit(solution)/shard_map/psum | solution.py:12
  688.7 1.7 fusion.37
  690.5 11.7 %cholesky.342 = f32[128,128]{1,0:T(8,128)S(1)} custom-call(f32[128,128]{1,0:T(8,128)S(1)} %cholesky.385), custom_call_target="Cholesky" | custom-call | tf_op jit(solution)/shard_map/jit(cholesky)/cholesky | solution.py:17
  702.3 9.8 %custom-call.25 = f32[1,128,128]{1,2,0:T(8,128)S(1)} custom-call(f32[1,128,128]{2,1,0:T(8,128)S(1)} %get-tuple-element.94), custom_call_target="InvertDiagBlocksLowerTriangular" | custom-call | tf_op jit(solution)/shard_map/jit(cholesky)/cholesky | solution.py:17
  712.5 5.8 cholesky.362
  721.1 19.9 %custom-call.26 = f32[2,128,128]{1,2,0:T(8,128)S(1)} custom-call(f32[2,128,128]{2,1,0:T(8,128)S(1)} %pad_maximum_fusion.3), custom_call_target="InvertDiagBlocksLowerTriangular" | custom-call | tf_op jit(solution)/shard_map/jit(_cho_solve)/triangular_solve | solution.py:18
  742.8 2.6 convolution_select_fusion
  745.6 42.8 %all-reduce.29.cloned.1.call-done = f32[1536,192]{1,0:T(8,128)} async-done(((f32[1536,192]{1,0:T(8,128)}), f32[1536,192]{1,0:T(8,128)}) %all-reduce.29.cloned.1.call-update) | async-done | bytes 1179664 | tf_op jit(solution)/shard_map/psum | solution.py:12
  788.4 7.5 select_subtract_fusion
  795.9 2.2 copy-done.6
  798.1 2.1 select_select_fusion
  800.2 8.6 %scatter.19 = f32[1536,768]{1,0:T(8,128)} dynamic-update-slice(f32[1536,768]{1,0:T(8,128)} %copy-done.6, f32[1536,192]{1,0:T(8,128)} %select_select_fusion, s32[]{:T(128)} %constant.195.clone.1, s32[]{:T(128)} %constant.195.clone.1) | dynamic-update-slice | bytes 2359300 | tf_op jit(solution)/shard_map/scatter | solution.py:72
  (169 shorter events, 17.5 us)
Async XLA Ops:
  6.5 17.9 %copy-start = (bf16[1536,768]{1,0:T(8,128)(2,1)S(1)}, bf16[1536,768]{1,0:T(8,128)(2,1)}, u32[]{:S(2)}) copy-start(bf16[1536,768]{1,0:T(8,128)(2,1)} %param.16) | copy-start | bytes 7077892
  6.5 192.7 %all-reduce.13.cloned.1.call-start = ((), (), s32[]{:S(2)}) async-start(), calls=%async_computation | async-start | bytes 9437184 | tf_op jit(solution)/shard_map/psum | solution.py:50
  12.2 7.2 copy-start.15
  24.4 210.6 %all-reduce.15.cloned.1.call-start = ((), (), s32[]{:S(2)}) async-start(), calls=%async_computation.1 | async-start | bytes 1179648 | tf_op jit(solution)/shard_map/psum | solution.py:12
  202.8 2.2 copy-start.5
  205.8 130.6 %all-reduce.17.cloned.1.call-start = ((), (), s32[]{:S(2)}) async-start(), calls=%async_computation.2 | async-start | bytes 3145728 | tf_op jit(solution)/shard_map/psum | solution.py:12
  235.0 52.6 %copy-start.11 = (f32[192,768]{1,0:T(8,128)S(1)}, f32[192,768]{1,0:T(8,128)}, u32[]{:S(2)}) copy-start(f32[192,768]{1,0:T(8,128)} %all-reduce.15.cloned.1.call-done) | copy-start | bytes 1769476
  293.4 93.9 %all-reduce.19.cloned.1.call-start = ((), (), s32[]{:S(2)}) async-start(), calls=%async_computation.3 | async-start | bytes 1179648 | tf_op jit(solution)/shard_map/psum | solution.py:12
  336.4 9.7 %copy-start.7 = (f32[1536,192]{1,0:T(8,128)S(1)}, f32[1536,192]{1,0:T(8,128)}, u32[]{:S(2)}) copy-start(f32[1536,192]{1,0:T(8,128)} %all-reduce.17.cloned.1.call-done) | copy-start | bytes 3538948
  343.9 2.2 copy-start.2
  357.0 130.0 %all-reduce.21.cloned.1.call-start = ((), (), s32[]{:S(2)}) async-start(), calls=%async_computation.4 | async-start | bytes 3145728 | tf_op jit(solution)/shard_map/psum | solution.py:12
  387.3 52.3 %copy-start.13 = (f32[192,768]{1,0:T(8,128)S(1)}, f32[192,768]{1,0:T(8,128)}, u32[]{:S(2)}) copy-start(f32[192,768]{1,0:T(8,128)} %all-reduce.19.cloned.1.call-done) | copy-start | bytes 1769476
  444.0 93.8 %all-reduce.23.cloned.1.call-start = ((), (), s32[]{:S(2)}) async-start(), calls=%async_computation.5 | async-start | bytes 1179648 | tf_op jit(solution)/shard_map/psum | solution.py:12
  487.0 9.7 %copy-start.8 = (f32[1536,192]{1,0:T(8,128)S(1)}, f32[1536,192]{1,0:T(8,128)}, u32[]{:S(2)}) copy-start(f32[1536,192]{1,0:T(8,128)} %all-reduce.21.cloned.1.call-done) | copy-start | bytes 3538948
  494.5 2.2 copy-start.3
  507.6 130.2 %all-reduce.25.cloned.1.call-start = ((), (), s32[]{:S(2)}) async-start(), calls=%async_computation.6 | async-start | bytes 3145728 | tf_op jit(solution)/shard_map/psum | solution.py:12
  537.9 52.6 %copy-start.14 = (f32[192,768]{1,0:T(8,128)S(1)}, f32[192,768]{1,0:T(8,128)}, u32[]{:S(2)}) copy-start(f32[192,768]{1,0:T(8,128)} %all-reduce.23.cloned.1.call-done) | copy-start | bytes 1769476
  594.8 93.9 %all-reduce.27.cloned.1.call-start = ((), (), s32[]{:S(2)}) async-start(), calls=%async_computation.7 | async-start | bytes 1179648 | tf_op jit(solution)/shard_map/psum | solution.py:12
  637.8 9.7 %copy-start.9 = (f32[1536,192]{1,0:T(8,128)S(1)}, f32[1536,192]{1,0:T(8,128)}, u32[]{:S(2)}) copy-start(f32[1536,192]{1,0:T(8,128)} %all-reduce.25.cloned.1.call-done) | copy-start | bytes 3538948
  645.3 2.2 copy-start.4
  658.4 130.0 %all-reduce.29.cloned.1.call-start = ((), (), s32[]{:S(2)}) async-start(), calls=%async_computation.8 | async-start | bytes 3145728 | tf_op jit(solution)/shard_map/psum | solution.py:12
  688.7 52.3 %copy-start.12 = (f32[192,768]{1,0:T(8,128)S(1)}, f32[192,768]{1,0:T(8,128)}, u32[]{:S(2)}) copy-start(f32[192,768]{1,0:T(8,128)} %all-reduce.27.cloned.1.call-done) | copy-start | bytes 1769476
  788.4 9.7 %copy-start.10 = (f32[1536,192]{1,0:T(8,128)S(1)}, f32[1536,192]{1,0:T(8,128)}, u32[]{:S(2)}) copy-start(f32[1536,192]{1,0:T(8,128)} %all-reduce.29.cloned.1.call-done) | copy-start | bytes 3538948
  795.9 2.2 copy-start.6
  798.1 10.7 %copy-start.1 = (bf16[1536,768]{1,0:T(8,128)(2,1)S(1)}, bf16[1536,768]{1,0:T(8,128)(2,1)}, u32[]{:S(2)}) copy-start(bf16[1536,768]{1,0:T(8,128)(2,1)} %param.16) | copy-start | bytes 7077892
Sparse Core Ops, SparseCore 0:
  24.5 174.6 all-reduce.12
  205.9 29.0 all-reduce.14
  293.5 42.8 all-reduce.16
  357.1 30.1 all-reduce.18
  444.1 42.8 all-reduce.20
  507.7 30.0 all-reduce.22
  594.9 42.8 all-reduce.24
  658.5 30.1 all-reduce.26
  745.5 42.8 all-reduce.28
where the time goes:
time: 820 us; the launch traced here: 816 us
  waiting for transfers between devices  458 us (56%)
  other arithmetic  216 us (26%)
  matrix products  61.6 us (8%)
  local copies, waits for them, and re-layouts  59.1 us (7%)
  between operations  19.3 us (2%)
    psum x8, waiting for transfers between devices, broadcast(): return lax.psum(block, axis)  289 us
    psum x1, waiting for transfers between devices, shards(): panel_work = front_sorted - lax.psum(partial_value, 'layer')  169 us
    another operation x28, other arithmetic, invert_block(): factor = jnp.linalg.cholesky(gram)  115 us
    another operation x18, other arithmetic, invert_block(): return jax.scipy.linalg.cho_solve((factor, True), diagonal.T)  80.6 us
    scatter x4, local copies, waits for them, and re-layouts, shards(): panel_work = panel_work.at[:, col_start:col_start + block_size].set(placed)  33 us
    dot_general x4, matrix products, shards(): product = jnp.dot(lower_part, upper_row, precision=PRECISE)  29.9 us
  transfers between devices with their start and end apart: 9, of which 9 were waited for; matrix products, arithmetic and copies ran while one was open for 1% of the time, Pallas kernels for 0%

commit v1 on v0

--- a/solution.py
+++ b/solution.py
@@ -47,7 +47,8 @@
     )
     identity = jnp.eye(block_size, dtype=jnp.float32)
     partial_value = jnp.dot(lower_sorted, upper_masked, preferred_element_type=jnp.float32)
-    panel_work = front_sorted - lax.psum(partial_value, "layer")
+    map_signs_for = lambda mine_x: jnp.sum(lax.all_gather(mine_x, "layer"), 0)
+    panel_work = front_sorted - map_signs_for(partial_value)
     for step_index in range(step_count):
         root_row = step_index % grid_rows
         root_col = step_index % grid_cols

time: 820 us -> 962 us (1.17)
  waiting for transfers between devices: 458 us -> 601 us
  local copies, waits for them, and re-layouts: 59.1 us -> 45.3 us
  other arithmetic: 216 us -> 226 us
    all_gather x0 -> x1, waiting for transfers between devices: none -> 317 us  [shards(): map_signs_for = lambda mine_x: jnp.sum(lax.all_gather(mine_x, 'layer'), 0)]
    psum x1 -> x0, waiting for transfers between devices: 169 us -> none  [shards(): panel_work = front_sorted - lax.psum(partial_value, 'layer')]
    scatter x4 -> x1, local copies, waits for them, and re-layouts: 33 us -> 6.19 us  [shards(): panel_work = panel_work.at[:, col_start:col_start + block_size].set(placed)]
    reduce_sum x0 -> x1, other arithmetic: none -> 10.4 us  [shards(): map_signs_for = lambda mine_x: jnp.sum(lax.all_gather(mine_x, 'layer'), 0)]
where the time goes in v1:
time: 962 us; the launch traced here: 956 us
  waiting for transfers between devices  601 us (62%)
  other arithmetic  226 us (23%)
  matrix products  63.3 us (7%)
  local copies, waits for them, and re-layouts  45.3 us (5%)
  between operations  19.3 us (2%)
    all_gather x1, waiting for transfers between devices, shards(): map_signs_for = lambda mine_x: jnp.sum(lax.all_gather(mine_x, 'layer'), 0)  317 us
    psum x8, waiting for transfers between devices, broadcast(): return lax.psum(block, axis)  284 us
    another operation x28, other arithmetic, invert_block(): factor = jnp.linalg.cholesky(gram)  115 us
    another operation x18, other arithmetic, invert_block(): return jax.scipy.linalg.cho_solve((factor, True), diagonal.T)  80.6 us
    dot_general x4, matrix products, shards(): product = jnp.dot(lower_part, upper_row, precision=PRECISE)  27.4 us
  transfers between devices with their start and end apart: 9, of which 9 were waited for; matrix products, arithmetic and copies ran while one was open for 1% of the time, Pallas kernels for 0%

profile of v1, /device:TPU:0, one launch (start us, length us, event | category | flops | bytes accessed | tf_op | source)
XLA Modules:
  0.0 955.5 jit_solution(5311723145706634508)
XLA Ops:
  6.5 0.9 fusion.94
  7.6 0.7 fusion.92
  8.5 0.8 broadcast_add_fusion
  9.4 2.8 broadcast_multiply_fusion
  12.2 7.2 gather_fusion.1
  19.4 5.0 fusion.4
  24.5 5.6 gather_fusion
  30.1 2.8 copy.12
  32.9 316.9 %all-gather.3.cloned.1.call-done = f32[6144,768]{1,0:T(8,128)} async-done(((f32[1536,768]{1,0:T(8,128)}), f32[6144,768]{1,0:T(8,128)}) %all-gather.3.cloned.1.call-update) | async-done | bytes 18874384 | tf_op jit(solution)/shard_map/all_gather | solution.py:50
  349.8 10.4 %reduce_sum.9 = f32[1536,768]{1,0:T(8,128)} reduce(f32[4,1536,768]{2,1,0:T(8,128)} %bitcast.142, f32[]{:T(128)} %constant.205.clone.1), dimensions={0}, to_apply=%region_0.0 | reduce | flops 3538944 | bytes 23592964 | tf_op jit(solution)/shard_map/reduce_sum | solution.py:50
  360.2 6.0 copy.13
  366.3 3.0 convert_subtract_fusion
  369.3 2.2 copy-done.5
  371.5 1.0 slice_select_fusion.5
  373.1 32.8 %all-reduce.12.cloned.1.call-done = f32[192,768]{0,1:T(8,128)} async-done(((f32[192,768]{0,1:T(8,128)}), f32[192,768]{0,1:T(8,128)}) %all-reduce.12.cloned.1.call-update) | async-done | bytes 589840 | tf_op jit(solution)/shard_map/psum | solution.py:12
  405.8 1.4 fusion.35
  407.4 11.7 %cholesky.228 = f32[128,128]{1,0:T(8,128)S(1)} custom-call(f32[128,128]{1,0:T(8,128)S(1)} %cholesky.376), custom_call_target="Cholesky" | custom-call | tf_op jit(solution)/shard_map/jit(cholesky)/cholesky | solution.py:17
  419.2 9.8 %custom-call.19 = f32[1,128,128]{1,2,0:T(8,128)S(1)} custom-call(f32[1,128,128]{2,1,0:T(8,128)S(1)} %get-tuple-element.100), custom_call_target="InvertDiagBlocksLowerTriangular" | custom-call | tf_op jit(solution)/shard_map/jit(cholesky)/cholesky | solution.py:17
  429.4 5.8 cholesky.248
  437.9 20.2 %custom-call.20 = f32[2,128,128]{1,2,0:T(8,128)S(1)} custom-call(f32[2,128,128]{2,1,0:T(8,128)S(1)} %pad_maximum_fusion), custom_call_target="InvertDiagBlocksLowerTriangular" | custom-call | tf_op jit(solution)/shard_map/jit(_cho_solve)/triangular_solve | solution.py:18
  460.1 3.5 convolution_select_fusion.3
  464.5 36.6 %all-reduce.14.cloned.1.call-done = f32[1536,192]{0,1:T(8,128)} async-done(((f32[1536,192]{0,1:T(8,128)}), f32[1536,192]{0,1:T(8,128)}) %all-reduce.14.cloned.1.call-update) | async-done | bytes 1179664 | tf_op jit(solution)/shard_map/psum | solution.py:12
  501.1 6.4 select_subtract_fusion.3
  507.9 1.8 copy-done.8
  509.7 1.0 fusion.15
  510.7 2.2 copy-done.2
  512.9 1.0 slice_select_fusion.4
  514.3 34.3 %all-reduce.16.cloned.1.call-done = f32[192,768]{0,1:T(8,128)} async-done(((f32[192,768]{0,1:T(8,128)}), f32[192,768]{0,1:T(8,128)}) %all-reduce.16.cloned.1.call-update) | async-done | bytes 589840 | tf_op jit(solution)/shard_map/psum | solution.py:12
  548.6 1.4 fusion.37
  550.2 11.7 %cholesky.266 = f32[128,128]{1,0:T(8,128)S(1)} custom-call(f32[128,128]{1,0:T(8,128)S(1)} %cholesky.379), custom_call_target="Cholesky" | custom-call | tf_op jit(solution)/shard_map/jit(cholesky)/cholesky | solution.py:17
  562.0 9.8 %custom-call.21 = f32[1,128,128]{1,2,0:T(8,128)S(1)} custom-call(f32[1,128,128]{2,1,0:T(8,128)S(1)} %get-tuple-element.98), custom_call_target="InvertDiagBlocksLowerTriangular" | custom-call | tf_op jit(solution)/shard_map/jit(cholesky)/cholesky | solution.py:17
  572.2 5.8 cholesky.286
  580.8 19.9 %custom-call.22 = f32[2,128,128]{1,2,0:T(8,128)S(1)} custom-call(f32[2,128,128]{2,1,0:T(8,128)S(1)} %pad_maximum_fusion.1), custom_call_target="InvertDiagBlocksLowerTriangular" | custom-call | tf_op jit(solution)/shard_map/jit(_cho_solve)/triangular_solve | solution.py:18
  602.6 4.3 convolution_select_fusion.2
  607.1 37.2 %all-reduce.18.cloned.1.call-done = f32[1536,192]{0,1:T(8,128)} async-done(((f32[1536,192]{0,1:T(8,128)}), f32[1536,192]{0,1:T(8,128)}) %all-reduce.18.cloned.1.call-update) | async-done | bytes 1179664 | tf_op jit(solution)/shard_map/psum | solution.py:12
  644.3 6.4 select_subtract_fusion.2
  651.1 1.8 copy-done.7
  652.9 1.0 fusion.16
  653.9 2.2 copy-done.3
  656.1 1.2 slice_select_fusion.3
  657.8 34.1 %all-reduce.20.cloned.1.call-done = f32[192,768]{0,1:T(8,128)} async-done(((f32[192,768]{0,1:T(8,128)}), f32[192,768]{0,1:T(8,128)}) %all-reduce.20.cloned.1.call-update) | async-done | bytes 589840 | tf_op jit(solution)/shard_map/psum | solution.py:12
  691.9 1.4 fusion.39
  693.6 11.7 %cholesky.304 = f32[128,128]{1,0:T(8,128)S(1)} custom-call(f32[128,128]{1,0:T(8,128)S(1)} %cholesky.382), custom_call_target="Cholesky" | custom-call | tf_op jit(solution)/shard_map/jit(cholesky)/cholesky | solution.py:17
  705.3 9.8 %custom-call.23 = f32[1,128,128]{1,2,0:T(8,128)S(1)} custom-call(f32[1,128,128]{2,1,0:T(8,128)S(1)} %get-tuple-element.96), custom_call_target="InvertDiagBlocksLowerTriangular" | custom-call | tf_op jit(solution)/shard_map/jit(cholesky)/cholesky | solution.py:17
  715.5 5.8 cholesky.324
  724.1 20.1 %custom-call.24 = f32[2,128,128]{1,2,0:T(8,128)S(1)} custom-call(f32[2,128,128]{2,1,0:T(8,128)S(1)} %pad_maximum_fusion.2), custom_call_target="InvertDiagBlocksLowerTriangular" | custom-call | tf_op jit(solution)/shard_map/jit(_cho_solve)/triangular_solve | solution.py:18
  746.2 4.3 convolution_select_fusion.1
  750.7 37.2 %all-reduce.22.cloned.1.call-done = f32[1536,192]{0,1:T(8,128)} async-done(((f32[1536,192]{0,1:T(8,128)}), f32[1536,192]{0,1:T(8,128)}) %all-reduce.22.cloned.1.call-update) | async-done | bytes 1179664 | tf_op jit(solution)/shard_map/psum | solution.py:12
  787.9 6.4 select_subtract_fusion.1
  794.6 1.8 copy-done.6
  796.4 1.0 fusion.17
  797.5 2.2 copy-done.4
  799.6 1.2 slice_select_fusion.2
  801.3 34.3 %all-reduce.24.cloned.1.call-done = f32[192,768]{0,1:T(8,128)} async-done(((f32[192,768]{0,1:T(8,128)}), f32[192,768]{0,1:T(8,128)}) %all-reduce.24.cloned.1.call-update) | async-done | bytes 589840 | tf_op jit(solution)/shard_map/psum | solution.py:12
  835.5 1.4 fusion.41
  837.2 11.7 %cholesky.342 = f32[128,128]{1,0:T(8,128)S(1)} custom-call(f32[128,128]{1,0:T(8,128)S(1)} %cholesky.385), custom_call_target="Cholesky" | custom-call | tf_op jit(solution)/shard_map/jit(cholesky)/cholesky | solution.py:17
  848.9 9.8 %custom-call.25 = f32[1,128,128]{1,2,0:T(8,128)S(1)} custom-call(f32[1,128,128]{2,1,0:T(8,128)S(1)} %get-tuple-element.94), custom_call_target="InvertDiagBlocksLowerTriangular" | custom-call | tf_op jit(solution)/shard_map/jit(cholesky)/cholesky | solution.py:17
  859.1 5.8 cholesky.362
  867.7 19.9 %custom-call.26 = f32[2,128,128]{1,2,0:T(8,128)S(1)} custom-call(f32[2,128,128]{2,1,0:T(8,128)S(1)} %pad_maximum_fusion.3), custom_call_target="InvertDiagBlocksLowerTriangular" | custom-call | tf_op jit(solution)/shard_map/jit(_cho_solve)/triangular_solve | solution.py:18
  889.5 4.3 convolution_select_fusion
  894.0 37.3 %all-reduce.26.cloned.1.call-done = f32[1536,192]{0,1:T(8,128)} async-done(((f32[1536,192]{0,1:T(8,128)}), f32[1536,192]{0,1:T(8,128)}) %all-reduce.26.cloned.1.call-update) | async-done | bytes 1179664 | tf_op jit(solution)/shard_map/psum | solution.py:12
  931.2 8.3 select_subtract_fusion
  939.5 3.1 fusion
  942.6 6.2 copy.18
  (176 shorter events, 20.5 us)
Async XLA Ops:
  6.5 17.9 %copy-start = (bf16[1536,768]{1,0:T(8,128)(2,1)S(1)}, bf16[1536,768]{1,0:T(8,128)(2,1)}, u32[]{:S(2)}) copy-start(bf16[1536,768]{1,0:T(8,128)(2,1)} %param.16) | copy-start | bytes 7077892
  6.5 343.3 %all-gather.3.cloned.1.call-start = ((), (), s32[]{:S(2)}) async-start(), calls=%async_computation.8 | async-start | bytes 23592960 | tf_op jit(solution)/shard_map/all_gather | solution.py:50
  12.2 7.2 copy-start.17
  24.4 381.4 %all-reduce.12.cloned.1.call-start = ((), (), s32[]{:S(2)}) async-start(), calls=%async_computation | async-start | bytes 1572864 | tf_op jit(solution)/shard_map/psum | solution.py:12
  369.3 2.2 copy-start.5
  372.5 128.6 %all-reduce.14.cloned.1.call-start = ((), (), s32[]{:S(2)}) async-start(), calls=%async_computation.1 | async-start | bytes 2359296 | tf_op jit(solution)/shard_map/psum | solution.py:12
  405.8 52.3 %copy-start.13 = (f32[192,768]{0,1:T(8,128)S(1)}, f32[192,768]{0,1:T(8,128)}, u32[]{:S(2)}) copy-start(f32[192,768]{0,1:T(8,128)} %all-reduce.12.cloned.1.call-done) | copy-start | bytes 1769476
  463.6 85.0 %all-reduce.16.cloned.1.call-start = ((), (), s32[]{:S(2)}) async-start(), calls=%async_computation.2 | async-start | bytes 1572864 | tf_op jit(solution)/shard_map/psum | solution.py:12
  507.5 2.1 copy-start.8
  507.6 2.1 copy-start.10
  510.7 2.2 copy-start.2
  513.9 130.4 %all-reduce.18.cloned.1.call-start = ((), (), s32[]{:S(2)}) async-start(), calls=%async_computation.3 | async-start | bytes 2359296 | tf_op jit(solution)/shard_map/psum | solution.py:12
  548.6 52.1 %copy-start.15 = (f32[192,768]{0,1:T(8,128)S(1)}, f32[192,768]{0,1:T(8,128)}, u32[]{:S(2)}) copy-start(f32[192,768]{0,1:T(8,128)} %all-reduce.16.cloned.1.call-done) | copy-start | bytes 1769476
  606.9 85.1 %all-reduce.20.cloned.1.call-start = ((), (), s32[]{:S(2)}) async-start(), calls=%async_computation.4 | async-start | bytes 1572864 | tf_op jit(solution)/shard_map/psum | solution.py:12
  650.7 2.1 copy-start.7
  650.7 2.1 copy-start.11
  653.9 2.2 copy-start.3
  657.3 130.6 %all-reduce.22.cloned.1.call-start = ((), (), s32[]{:S(2)}) async-start(), calls=%async_computation.5 | async-start | bytes 2359296 | tf_op jit(solution)/shard_map/psum | solution.py:12
  691.9 52.3 %copy-start.16 = (f32[192,768]{0,1:T(8,128)S(1)}, f32[192,768]{0,1:T(8,128)}, u32[]{:S(2)}) copy-start(f32[192,768]{0,1:T(8,128)} %all-reduce.20.cloned.1.call-done) | copy-start | bytes 1769476
  750.4 85.1 %all-reduce.24.cloned.1.call-start = ((), (), s32[]{:S(2)}) async-start(), calls=%async_computation.6 | async-start | bytes 1572864 | tf_op jit(solution)/shard_map/psum | solution.py:12
  794.3 2.1 copy-start.6
  794.3 2.1 copy-start.9
  797.4 2.2 copy-start.4
  800.9 130.4 %all-reduce.26.cloned.1.call-start = ((), (), s32[]{:S(2)}) async-start(), calls=%async_computation.7 | async-start | bytes 2359296 | tf_op jit(solution)/shard_map/psum | solution.py:12
  835.5 52.1 %copy-start.14 = (f32[192,768]{0,1:T(8,128)S(1)}, f32[192,768]{0,1:T(8,128)}, u32[]{:S(2)}) copy-start(f32[192,768]{0,1:T(8,128)} %all-reduce.24.cloned.1.call-done) | copy-start | bytes 1769476
  931.2 8.3 copy-start.12
  942.6 6.2 copy-start.1
Sparse Core Ops, SparseCore 0:
  24.5 325.2 all-gather.2
  372.6 33.1 all-reduce.11
  463.7 37.3 all-reduce.13
  514.1 34.5 all-reduce.15
  607.0 37.2 all-reduce.17
  657.4 34.4 all-reduce.19
  750.6 37.2 all-reduce.21
  801.0 34.5 all-reduce.23
  893.9 37.2 all-reduce.25
